TPU v7x, 128 devices: a whole 4x4x4 slice. The times are simulated.
128 devices in a mesh: seq: 8 (over z, core), tp: 16 (over x, y).
Axes of the slice: x: 4, y: 4, z: 4, core: 2. Of those that a mesh axis runs over, the one named last changes fastest.
Arguments:
- new_tokens: bfloat16 [64, 8, 8192], P(None, 'seq'), may hold values from -6 to 6
- norm_gain: float32 [8192], replicated, may hold values from 0.5 to 1.5
- query_weight: bfloat16 [8192, 8192], P(None, 'tp'), may hold values from -1 to 1
- key_weight: bfloat16 [8192, 1024], P(None, 'tp'), may hold values from -1 to 1
- value_weight: bfloat16 [8192, 1024], P(None, 'tp'), may hold values from -0.0625 to 0.0625
- kv_cache: bfloat16 [2, 8, 32768, 1024], P(None, None, ('seq', 'tp')), may hold values from -20 to 20, as said below
- kept_blocks: int32 [8, 8, 256], replicated, may hold values from 0 to 511, as said below
- kept_counts: int32 [8, 8], replicated, may hold values from 2 to 256, as said below
Outputs:
- attended: bfloat16 [64, 8, 8192], P(None, 'seq', 'tp')
- new_entries: bfloat16 [8, 16, 16384], P('seq', 'tp')
Inputs may be any that keep to these rules, and one draw needn't show every extreme that they name: `kv_cache`: index 0 of the first dimension holds keys, index 1 values. `kept_blocks`: for each prompt and KV head the first kept_counts entries are distinct block numbers in ascending order and the rest are 0. Among the 4 blocks of a prompt that one device of seq+tp holds, at most 2 are kept for one KV head; in every draw some prompt and head keeps exactly 2 on every device, and every prompt and head keeps exactly 2 on some device. `kept_counts`: the number of valid entries of kept_blocks for each prompt and KV head.
All inputs are finite; a program needn't handle non-finite values.
Results may differ from a plain program's by a relative error of at most 0.012.
Values may be sent and summed in bfloat16 or wider, within the bound.
A program may use at most 128 MiB of HBM per device.

v0:
```python
import math

import jax
import jax.numpy as jnp
from jax import lax
from jax.sharding import PartitionSpec as P

KVH = 8
HD = 128
BLOCK = 64
CAP = 2


def partner_2(value, axis, apart):
    return lax.ppermute(value, axis, [(i, i ^ 1 << apart) for i in range(lax.axis_size(axis))])


def scaled_norm(tokens, norm_gain):
    values = tokens.astype(jnp.float32)
    mean_square = jnp.mean(values * values, axis=-1, keepdims=True)
    return (values * lax.rsqrt(mean_square + 1e-05) * norm_gain).astype(jnp.bfloat16)


def per_device(
    new_tokens,
    norm_gain,
    query_weight,
    key_weight,
    value_weight,
    kv_cache,
    kept_blocks,
    kept_counts,
):
    n_seq = lax.axis_size("seq")
    n_tp = lax.axis_size("tp")
    devices = n_seq * n_tp
    copies = n_tp // KVH
    member = lax.axis_index("tp") % copies
    head_index = lax.axis_index("tp") // copies
    seq_index = lax.axis_index("seq")
    flat_index = lax.axis_index(("seq", "tp"))
    step_count, prompts_here, model_width = new_tokens.shape
    local_heads = query_weight.shape[1] // HD
    score_scale = 1.0 / math.sqrt(HD)
    normed = scaled_norm(new_tokens, norm_gain).reshape(step_count * prompts_here, model_width)
    queries = jnp.dot(normed, query_weight, preferred_element_type=jnp.float32).astype(jnp.bfloat16)
    queries = queries.reshape(step_count, prompts_here, local_heads, HD)
    key_piece = jnp.dot(normed, key_weight, preferred_element_type=jnp.float32).astype(jnp.bfloat16)
    value_piece = jnp.dot(normed, value_weight, preferred_element_type=jnp.float32).astype(
        jnp.bfloat16
    )
    pieces = jnp.stack([key_piece, value_piece])
    partner = partner_2(pieces, "tp", 0)
    fresh_rows = jnp.where(
        member == 0, jnp.concatenate([pieces, partner], 2), jnp.concatenate([partner, pieces], 2)
    )
    fresh_rows = fresh_rows.reshape(2, step_count, prompts_here, HD)
    new_entries = fresh_rows.transpose(2, 0, 1, 3).reshape(prompts_here, 1, 2 * step_count * HD)
    total_prompts, kv_heads, keep_slots = kept_blocks.shape
    blocks_here = kv_cache.shape[2] // BLOCK
    live_mask = jnp.arange(keep_slots, dtype=jnp.int32)[None, None, :] < kept_counts[:, :, None]
    wanted = flat_index * blocks_here + jnp.arange(blocks_here, dtype=jnp.int32)
    chosen = jnp.any((kept_blocks[:, :, :, None] == wanted) & live_mask[:, :, :, None], axis=2)
    slot_rank = jnp.cumsum(chosen.astype(jnp.int32), axis=2) - 1
    slots_each = CAP
    picker = (
        (slot_rank[..., None] == jnp.arange(CAP, dtype=jnp.int32)) & chosen[..., None]
    ).astype(jnp.bfloat16)
    picker = picker.reshape(
        n_seq, prompts_here, kv_heads, blocks_here, CAP // slots_each, slots_each
    )
    cache_blocks = kv_cache.reshape(2, n_seq, prompts_here, blocks_here, BLOCK, kv_heads, HD)
    packed = jnp.einsum(
        "sphjrc,kspjthd->shrkpctd", picker, cache_blocks, preferred_element_type=jnp.float32
    ).astype(jnp.bfloat16)
    packed = jnp.broadcast_to(
        packed, (n_seq, kv_heads, copies, 2, prompts_here, slots_each, BLOCK, HD)
    )
    arrived = lax.all_to_all(
        packed.reshape(devices, 2, prompts_here, slots_each, BLOCK, HD),
        ("seq", "tp"),
        split_axis=0,
        concat_axis=0,
        tiled=True,
    )
    my_lists = lax.dynamic_slice(
        kept_blocks, (seq_index * prompts_here, head_index, 0), (prompts_here, 1, keep_slots)
    )[:, 0]
    my_counts = lax.dynamic_slice(
        kept_counts, (seq_index * prompts_here, head_index), (prompts_here, 1)
    )[:, 0]
    my_live = jnp.arange(keep_slots, dtype=jnp.int32)[None, :] < my_counts[:, None]
    source_of = my_lists // blocks_here
    per_source = jnp.sum(
        (
            (source_of[:, :, None] == jnp.arange(devices, dtype=jnp.int32)) & my_live[:, :, None]
        ).astype(jnp.int32),
        axis=1,
    )
    slot_live = jnp.arange(slots_each, dtype=jnp.int32)[None, None, :] < per_source[:, :, None]
    cache_keys = arrived[:, 0]
    cache_values = arrived[:, 1]
    cache_scores = (
        jnp.einsum("spgd,rpctd->psgrct", queries, cache_keys, preferred_element_type=jnp.float32)
        * score_scale
    )
    cache_scores = jnp.where(slot_live[:, None, None, :, :, None], cache_scores, -1e30)
    own_keys = fresh_rows[0]
    own_values = fresh_rows[1]
    own_scores = (
        jnp.einsum("spgd,upd->psgu", queries, own_keys, preferred_element_type=jnp.float32)
        * score_scale
    )
    causal = (
        jnp.arange(step_count, dtype=jnp.int32)[None, :]
        <= jnp.arange(step_count, dtype=jnp.int32)[:, None]
    )
    own_scores = jnp.where(causal[None, :, None, :], own_scores, -1e30)
    row_top = jnp.maximum(jnp.max(cache_scores, axis=(3, 4, 5)), jnp.max(own_scores, axis=3))
    cache_exp = jnp.exp(cache_scores - row_top[:, :, :, None, None, None])
    own_exp = jnp.exp(own_scores - row_top[:, :, :, None])
    row_total = jnp.sum(cache_exp, axis=(3, 4, 5)) + jnp.sum(own_exp, axis=3)
    cache_weights = (cache_exp / row_total[:, :, :, None, None, None]).astype(jnp.bfloat16)
    own_weights = (own_exp / row_total[:, :, :, None]).astype(jnp.bfloat16)
    head_output = jnp.einsum(
        "psgrct,rpctd->psgd", cache_weights, cache_values, preferred_element_type=jnp.float32
    )
    head_output = head_output + jnp.einsum(
        "psgu,upd->psgd", own_weights, own_values, preferred_element_type=jnp.float32
    )
    attended = (
        head_output.transpose(1, 0, 2, 3)
        .reshape(step_count, prompts_here, local_heads * HD)
        .astype(jnp.bfloat16)
    )
    return (attended, new_entries)


def solution(mesh):
    in_specs = (
        P(None, "seq", None),
        P(),
        P(None, "tp"),
        P(None, "tp"),
        P(None, "tp"),
        P(None, None, ("seq", "tp"), None),
        P(),
        P(),
    )
    out_specs = (P(None, "seq", "tp"), P("seq", "tp", None))
    return jax.shard_map(
        per_device, mesh=mesh, in_specs=in_specs, out_specs=out_specs, check_vma=False
    )
```

profile of v0, /device:TPU:1, one launch (start us, length us, event | category | flops | bytes accessed | tf_op | source)
XLA Modules:
  0.0 177.8 jit_solution(15148929807245559434)
XLA Ops:
  0.6 0.0 copy-start
  0.7 0.8 iota_compare_fusion.1
  1.5 1.5 and_reduce_fusion
  3.1 0.1 copy.31
  3.3 0.1 copy.30
  3.4 8.8 %copy.51 = bf16[512,8,8,128]{3,2,1,0:T(8,128)(2,1)} copy(bf16[512,8,8,128]{3,1,2,0:T(8,128)(2,1)} %bitcast.86) | data formatting | bytes 16777216
  12.2 8.5 %fusion.8 = bf16[8,8,2,2,64,128]{5,3,4,2,1,0:T(2,128)(2,1)S(1)} fusion(bf16[2,8,4,64,8,128]{5,4,3,2,1,0:T(8,128)(2,1)} %bitcast.87, pred[8,8,4]{2,1,0:T(8,128)(4,1)S(1)} %copy.31, s32[8,8,4]{2,1,0:T(8,128)S(1)} %copy.30), kind=kOutput, calls=%fused_computation.9 | convolution fusion | flops 18875392 | bytes 12584192 | tf_op jit(solution)/shard_map/sphjrc,kspjthd->shrkpctd/dot_general | solution.py:73
  20.7 1.2 copy.33
  21.9 5.4 %broadcast_in_dim.28 = bf16[8,8,2,2,2,64,128]{6,5,4,3,2,1,0:T(8,128)(2,1)} broadcast(bf16[8,8,2,2,64,128]{5,4,3,2,1,0:T(8,128)(2,1)S(1)} %copy.33), dimensions={0,1,3,4,5,6} | broadcast | bytes 12582912 | tf_op jit(solution)/shard_map/broadcast_in_dim | solution.py:76
  27.3 0.0 copy-start.2
  27.3 0.0 copy-start.3
  27.3 0.0 copy-start.4
  27.3 12.0 %all-to-all-start = ((bf16[128,2,1,2,64,128]{5,4,3,2,1,0:T(8,128)(2,1)}), bf16[128,2,1,2,64,128]{5,4,3,2,1,0:T(8,128)(2,1)}, u32[]{:S(2)}, u32[]{:S(2)}) async-start(bf16[128,2,1,2,64,128]{5,4,3,2,1,0:T(8,128)(2,1)} %bitcast.85), calls=%async_computation | async-start | bytes 16777216 | tf_op jit(solution)/shard_map/all_to_all | solution.py:79
  39.3 0.0 copy-done.2
  39.3 0.3 fusion.14
  39.6 0.0 copy-done
  39.6 0.0 copy-done.3
  39.6 0.5 fusion.27
  40.1 0.0 copy-done.4
  40.1 0.5 fusion.28
  40.7 1.5 collective-permute-start
  42.1 1.3 dynamic_slice.7
  43.4 0.6 iota_compare_fusion.3
  44.1 0.7 constant_dynamic-slice_fusion
  44.8 0.1 convert_reduce_fusion
  44.9 5.0 %convolution_convert_fusion = bf16[64,512]{1,0:T(8,128)(2,1)S(1)} fusion(bf16[8192,512]{1,0:T(8,128)(2,1)} %param.10, bf16[64,1,8192]{2,0,1:T(8,128)(2,1)S(1)} %copy-done.2, f32[8192]{0:T(1024)S(1)} %copy-done.3, f32[64]{0:T(128)S(1)} %add_rsqrt_fusion), kind=kOutput, calls=%fused_computation.24 | convolution fusion | flops 539000832 | bytes 9535744 | tf_op jit(solution)/shard_map/dot_general | solution.py:46
  50.0 85.7 %collective-permute-done = bf16[2,64,64]{2,1,0:T(8,128)(2,1)S(1)} collective-permute-done((bf16[2,64,64]{2,1,0:T(8,128)(2,1)S(1)}, bf16[2,64,64]{2,1,0:T(8,128)(2,1)S(1)}, u32[]{:S(2)}, u32[]{:S(2)}) %collective-permute-start) | collective-permute-done | bytes 16416 | tf_op jit(solution)/shard_map/ppermute | solution.py:15
  135.7 0.1 maximum_select_fusion
  135.8 0.6 select_n.67
  136.5 0.2 fusion.48
  136.7 3.4 %all-to-all-done = bf16[128,2,1,2,64,128]{5,4,3,2,1,0:T(8,128)(2,1)} async-done(((bf16[128,2,1,2,64,128]{5,4,3,2,1,0:T(8,128)(2,1)}), bf16[128,2,1,2,64,128]{5,4,3,2,1,0:T(8,128)(2,1)}, u32[]{:S(2)}, u32[]{:S(2)}) %all-to-all-start) | async-done | bytes 8388640 | tf_op jit(solution)/shard_map/all_to_all | solution.py:79
  140.1 5.0 %fusion.47 = (bf16[128,1,1,2,64,128]{5,4,3,2,1,0:T(8,128)(2,1)S(1)}, bf16[128,1,1,2,64,128]{5,4,3,2,1,0:T(8,128)(2,1)S(1)}) fusion(bf16[128,2,1,2,64,128]{5,4,3,2,1,0:T(8,128)(2,1)} %all-to-all-done), kind=kLoop, calls=%fused_computation.65 | loop fusion | bytes 16777216 | tf_op jit(solution)/shard_map/slice | solution.py:102
  145.1 8.2 %fusion = (f32[64,4]{0,1:T(4,128)S(1)}, f32[64,4,128,2,64]{2,0,4,3,1:T(8,128)}) fusion(pred[128,2]{0,1:T(4,128)(4,1)S(1)} %iota_compare_fusion.4, bf16[128,1,1,2,64,128]{5,4,3,2,1,0:T(8,128)(2,1)S(1)} %get-tuple-element.3, bf16[64,4,128,1,1]{2,1,0,4,3:T(4,128)(2,1)S(1)} %bitcast.88), kind=kOutput, calls=%fused_computation.3 | convolution fusion | flops 1086324480 | bytes 21038336 | tf_op jit(solution)/shard_map/spgd,rpctd->psgrct/dot_general | solution.py:104
  153.3 9.2 %fusion.1 = f32[64,4]{0,1:T(4,128)S(1)} fusion(f32[64,4,128,2,64]{2,0,4,3,1:T(8,128)} %get-tuple-element.5, f32[64,4]{0,1:T(4,128)S(1)} %max.13, pred[128,2]{0,1:T(4,128)(4,1)S(1)} %iota_compare_fusion.4), kind=kLoop, calls=%fused_computation.4 | loop fusion | flops 16776960 | bytes 16779520 | tf_op jit(solution)/shard_map/reduce_sum | solution.py:122
  162.5 0.2 fusion.39
  162.7 0.0 copy-start.1
  162.7 14.3 %fusion.24 = bf16[64,4,128]{2,0,1:T(8,128)(2,1)S(1)} fusion(f32[64,4,128]{2,0,1:T(8,128)S(1)} %fusion.39, bf16[128,1,1,2,64,128]{5,4,3,2,1,0:T(8,128)(2,1)S(1)} %get-tuple-element.2, f32[64,4,128,2,64]{2,0,4,3,1:T(8,128)} %get-tuple-element.5, f32[64,4]{0,1:T(4,128)S(1)} %add.74, f32[64,4]{0,1:T(4,128)S(1)} %max.13, pred[128,2]{0,1:T(4,128)(4,1)S(1)} %iota_compare_fusion.4), kind=kOutput, calls=%fused_computation.23 | convolution fusion | flops 1094778880 | bytes 21170432 | tf_op jit(solution)/shard_map/psgrct,rpctd->psgd/dot_general | solution.py:125
  177.0 0.1 copy.40
  177.1 0.7 convert_element_type.83
  177.8 0.0 copy-done.1
  (13 shorter events, 0.2 us)
Async XLA Ops:
  0.6 39.0 %copy-start = (bf16[8192,64]{0,1:T(8,128)(2,1)S(1)}, bf16[8192,64]{0,1:T(8,128)(2,1)}, u32[]{:S(2)}) copy-start(bf16[8192,64]{0,1:T(8,128)(2,1)} %param.11) | copy-start | bytes 3145732
  27.3 12.0 %copy-start.2 = (bf16[64,1,8192]{2,0,1:T(8,128)(2,1)S(1)}, bf16[64,1,8192]{2,0,1:T(8,128)(2,1)}, u32[]{:S(2)}) copy-start(bf16[64,1,8192]{2,0,1:T(8,128)(2,1)} %param.8) | copy-start | bytes 3145732
  27.3 12.3 %copy-start.3 = (f32[8192]{0:T(1024)S(1)}, f32[8192]{0:T(1024)}, u32[]{:S(2)}) copy-start(f32[8192]{0:T(1024)} %param.9) | copy-start | bytes 98308
  27.3 12.8 %copy-start.4 = (bf16[8192,64]{0,1:T(8,128)(2,1)S(1)}, bf16[8192,64]{0,1:T(8,128)(2,1)}, u32[]{:S(2)}) copy-start(bf16[8192,64]{0,1:T(8,128)(2,1)} %param.12) | copy-start | bytes 3145732
  27.3 112.8 %all-to-all-start = ((bf16[128,2,1,2,64,128]{5,4,3,2,1,0:T(8,128)(2,1)}), bf16[128,2,1,2,64,128]{5,4,3,2,1,0:T(8,128)(2,1)}, u32[]{:S(2)}, u32[]{:S(2)}) async-start(bf16[128,2,1,2,64,128]{5,4,3,2,1,0:T(8,128)(2,1)} %bitcast.85), calls=%async_computation | async-start | bytes 16777216 | tf_op jit(solution)/shard_map/all_to_all | solution.py:79
  40.7 95.1 %collective-permute-start = (bf16[2,64,64]{2,1,0:T(8,128)(2,1)S(1)}, bf16[2,64,64]{2,1,0:T(8,128)(2,1)S(1)}, u32[]{:S(2)}, u32[]{:S(2)}) collective-permute-start(bf16[2,64,64]{2,1,0:T(8,128)(2,1)S(1)} %pad_maximum_fusion), channel_id=1, source_target_pairs={{0,1},{1,0},{2,3},{3,2},{4,5},{5,4},{6,7},{7,6},{8,9},{9,8},{10,11... | collective-permute-start | bytes 49160 | tf_op jit(solution)/shard_map/ppermute | solution.py:15
  162.7 15.0 %copy-start.1 = (bf16[8192,64]{0,1:T(8,128)(2,1)S(1)}, bf16[8192,64]{0,1:T(8,128)(2,1)}, u32[]{:S(2)}) copy-start(bf16[8192,64]{0,1:T(8,128)(2,1)} %param.11) | copy-start | bytes 3145732
where the time goes:
time: 179 us; the launch traced here: 178 us
  waiting for transfers between devices  89.2 us (50%)
  matrix products  37.4 us (21%)
  local copies, waits for them, and re-layouts  24 us (13%)
  starting transfers between devices  13.4 us (7%)
  other arithmetic  12.9 us (7%)
    ppermute x1, waiting for transfers between devices, partner_2(): lax.ppermute(value, axis, [(i, i ^ 1 << apart) for i in range(lax.axis_si...  85.7 us
    dot_general x1, matrix products, per_device(): jnp.einsum('psgrct,rpctd->psgd', cache_weights, cache_values, preferred_e...  14.3 us
    all_to_all x1, starting transfers between devices, per_device(): lax.all_to_all(packed.reshape(devices, 2, prompts_here, slots_each, BLOCK...  12 us
    reduce_sum x2, other arithmetic, per_device(): row_total = jnp.sum(cache_exp, axis=(3, 4, 5)) + jnp.sum(own_exp, axis=3)  9.23 us
    unnamed x11, local copies, waits for them, and re-layouts  8.8 us
    dot_general x1, matrix products, per_device(): jnp.einsum('sphjrc,kspjthd->shrkpctd', picker, cache_blocks, preferred_el...  8.52 us
    dot_general x1, matrix products, per_device(): jnp.einsum('spgd,rpctd->psgrct', queries, cache_keys, preferred_element_t...  8.16 us
    broadcast_in_dim x2, local copies, waits for them, and re-layouts, per_device(): jnp.broadcast_to(packed, (n_seq, kv_heads, copies, 2, prompts_here, slots...  6.6 us
  transfers between devices with their start and end apart: 2, of which 2 were waited for; matrix products, arithmetic and copies ran while one was open for 6% of the time, Pallas kernels for 0%

commit v1 on v0

v1 whole, which is shorter than its diff:
```python
import math

import jax
import jax.numpy as jnp
from jax import lax
from jax.experimental import pallas as pl
from jax.experimental.pallas import tpu as pltpu
from jax.sharding import PartitionSpec as P

HD = 128
BLOCK = 64
CAP = 2
STEPS = 64
KEYS = CAP * BLOCK
TOKD = 256
WIDTH = 8192
SLOTS = 4
SOURCES = 16
SITES = 8
GROUP = 256
CHUNKS = 8
CHUNK = WIDTH // CHUNKS
MESH = pl.DeviceIdType.MESH
EXP_SCALE = math.log2(math.e) / math.sqrt(HD)
LOWEST = -1e30

NT = (((1,), (1,)), ((), ()))
TN = (((0,), (0,)), ((), ()))


def kernel(
    tok_hbm,
    gain_ref,
    wq_hbm,
    wk_hbm,
    wv_hbm,
    kv_hbm,
    kept_ref,
    counts_ref,
    att_ref,
    ent_ref,
    kv_buf,
    packed,
    recv,
    tok,
    normed,
    wq,
    wkv,
    q_acc,
    n_acc,
    q_send,
    q_buf,
    pick,
    live_keys,
    s_buf,
    p_buf,
    o_send,
    l_send,
    o_buf,
    l_buf,
    own_o,
    own_l,
    piece,
    other,
    kv_sem,
    w_sem,
    tok_sem,
    pack_sem,
    recv_sem,
    q_send_sem,
    q_recv_sem,
    o_send_sem,
    o_recv_sem,
    l_send_sem,
    l_recv_sem,
    piece_sem,
):
    seq = lax.axis_index("seq")
    tp = lax.axis_index("tp")
    z, c = seq // 2, seq % 2
    x, y = tp // 4, tp % 4
    flat = seq * 16 + tp

    def device(x_, y_, z_, c_):
        return (z_ * 2 + c_, x_ * 4 + y_)

    kv_copies = []
    for t in range(SLOTS):
        u, v = t // 2, t % 2
        kv_copies.append(
            pltpu.make_async_copy(
                kv_hbm.at[:, pl.ds(4 * u, 4), :, pl.ds(512 * v, 512)], kv_buf.at[t], kv_sem.at[t]
            )
        )
        kv_copies[t].start()
    tok_copy = pltpu.make_async_copy(tok_hbm, tok, tok_sem)
    wk_copy = pltpu.make_async_copy(wk_hbm, wkv.at[pl.ds(0, 64)], w_sem.at[CHUNKS])
    wv_copy = pltpu.make_async_copy(wv_hbm, wkv.at[pl.ds(64, 64)], w_sem.at[CHUNKS + 1])

    def wq_copy(k):
        rows = pl.ds(pl.multiple_of(k * CHUNK, CHUNK), CHUNK)
        return pltpu.make_async_copy(wq_hbm.at[rows], wq.at[rows], w_sem.at[k])

    barrier = pltpu.get_barrier_semaphore()

    def greet_near(i, carry):
        c_ = (c + i) % 2
        z_ = (z + (i // 2) % 3 + 3) % 4
        y_ = (y + (i // 6) % 3 + 3) % 4
        x_ = (x + i // 18 + 3) % 4

        @pl.when(i != 26)
        def _():
            pl.semaphore_signal(
                barrier, inc=1, device_id=device(x_, y_, z_, c_), device_id_type=MESH
            )

        return carry

    lax.fori_loop(0, 54, greet_near, 0)

    def greet_far(i, carry):
        y_ = (y + i % 4) % 4
        z_ = (z + 2 * ((i // 4) % 2)) % 4
        x_ = (x + 2 * (i // 8)) % 4
        pl.semaphore_signal(barrier, inc=1, device_id=device(x_, y_, z_, c), device_id_type=MESH)
        return carry

    lax.fori_loop(1, 16, greet_far, 0)

    lane = lax.broadcasted_iota(jnp.int32, (8, 256), 1)
    eye = lax.broadcasted_iota(jnp.int32, (8, 8), 0) == lax.broadcasted_iota(jnp.int32, (8, 8), 1)
    lane_8 = lax.broadcasted_iota(jnp.int32, (1, 8), 1)
    for p in range(8):
        count = jnp.sum(jnp.where(eye, counts_ref[pl.ds(p, 1), :], 0), axis=1, keepdims=True)
        rel = kept_ref[p] - 4 * flat
        code = jnp.where(rel == 0, 1, jnp.where(rel == 1, 2, jnp.where(rel == 2, 4, 8)))
        code = jnp.where((rel >= 0) & (rel < 4) & (lane < count), code, 0)
        mask = jnp.sum(code, axis=1, keepdims=True)
        h0, h1, h2 = mask & 1, (mask >> 1) & 1, (mask >> 2) & 1
        first = jnp.where(h0 == 1, 0, jnp.where(h1 == 1, 1, jnp.where(h2 == 1, 2, 3)))
        second = jnp.where(h0 + h1 == 2, 1, jnp.where((h0 + h1 == 1) & (h2 == 1), 2, 3))
        pick[0, pl.ds(8 * p, 8), :] = jnp.broadcast_to(first, (8, HD))
        pick[1, pl.ds(8 * p, 8), :] = jnp.broadcast_to(second, (8, HD))
    source = lax.broadcasted_iota(jnp.int32, (SOURCES, 256), 0)
    lane_16 = lax.broadcasted_iota(jnp.int32, (SOURCES, 256), 1)
    sx, sy = source >> 3, (source >> 2) & 1
    sz, sc = (source >> 1) & 1, source & 1
    for t in range(SLOTS):
        u, v = t // 2, t % 2
        ax, ay, az = (u + y) % 2, (v + z) % 2, (u + v + x) % 2
        nx = (x + 5 - 2 * ((x + ax) % 2)) % 4
        ny = (y + 5 - 2 * ((y + ay) % 2)) % 4
        nz = (z + 5 - 2 * ((z + az) % 2)) % 4
        fx = jnp.where(sx == 0, x, nx)
        fy = jnp.where(sy == 0, y, ny)
        fz = jnp.where(sz == 0, z, nz)
        fc = jnp.where(sc == 0, c, 1 - c)
        owner = (fz * 2 + fc) * 16 + fx * 4 + fy
        p_ = 2 * (2 * u + z % 2) + c
        h_ = 2 * (2 * v + x % 2) + (y + u + v) % 2
        row = kept_ref[p_, pl.ds(h_, 1), :]
        counts = jnp.where(lane_8 == h_, counts_ref[pl.ds(p_, 1), :], 0)
        live = lane_16 < jnp.sum(counts, axis=1, keepdims=True)
        here = jnp.where(live & ((row >> 2) == owner), 1, 0)
        live_keys[pl.ds(16 * t, 16), :] = jnp.broadcast_to(
            BLOCK * jnp.sum(here, axis=1, keepdims=True), (SOURCES, 2 * GROUP)
        )
    pl.semaphore_wait(barrier, 68)

    def pack(t, cls, dst):
        u, v = t // 2, t % 2
        rx = (x + cls // 8) % 2
        ry = (y + cls // 4) % 2
        rz = (z + cls // 2) % 2
        rc = (c + cls) % 2
        p_loc = 2 * rz + rc
        h_loc = 2 * rx + (ry + u + v) % 2
        pair = (4 * u + p_loc) * 8 + 4 * v + h_loc
        columns = pl.ds(pl.multiple_of(h_loc * HD, HD), HD)
        for slot in range(CAP):
            chosen = jnp.broadcast_to(pick[slot, pl.ds(pair, 1), :], (16, HD))
            part = [None, None]
            for block in range(slot, 4):
                weight = jnp.where(chosen == block, 1.0, 0.0).astype(jnp.bfloat16)
                weight = jnp.concatenate([weight] * (BLOCK // 16), axis=0)
                for kind in range(2):
                    rows = kv_buf[t, kind, p_loc, pl.ds(block * BLOCK, BLOCK), columns] * weight
                    part[kind] = rows if part[kind] is None else part[kind] + rows
            for kind in range(2):
                dst[kind, pl.ds(slot * BLOCK, BLOCK), :] = part[kind]

    for t in range(SLOTS):
        u, v = t // 2, t % 2
        kv_copies[t].wait()

        def send(cls, carry, t=t, u=u, v=v):
            dx, dy, dz, dc = cls // 8, (cls // 4) % 2, (cls // 2) % 2, cls % 2
            rx, ry, rz, rc = (x + dx) % 2, (y + dy) % 2, (z + dz) % 2, (c + dc) % 2
            ax, ay, az = (u + ry) % 2, (v + rz) % 2, (u + v + rx) % 2
            x_ = (x + dx * (1 - 2 * ((x + ax) % 2)) + 4) % 4
            y_ = (y + dy * (1 - 2 * ((y + ay) % 2)) + 4) % 4
            z_ = (z + dz * (1 - 2 * ((z + az) % 2)) + 4) % 4
            place = t * 15 + cls - 1
            pack(t, cls, packed.at[place])
            pltpu.make_async_remote_copy(
                src_ref=packed.at[place],
                dst_ref=recv.at[t, cls],
                send_sem=pack_sem,
                recv_sem=recv_sem.at[t],
                device_id=device(x_, y_, z_, rc),
                device_id_type=MESH,
            ).start()
            return carry

        lax.fori_loop(1, SOURCES, send, 0)
        if t == 0:
            tok_copy.start()
            wk_copy.start()
            wv_copy.start()
            for k in range(CHUNKS):
                wq_copy(k).start()
    for t in range(SLOTS):
        pack(t, 0, recv.at[t, 0])

    tok_copy.wait()

    def norm(i, carry):
        rows = pl.ds(pl.multiple_of(i * 16, 16), 16)
        values = tok[rows, :].astype(jnp.float32)
        mean_square = jnp.mean(values * values, axis=-1, keepdims=True)
        normed[rows, :] = (values * lax.rsqrt(mean_square + 1e-05) * gain_ref[...]).astype(
            jnp.bfloat16
        )
        return carry

    lax.fori_loop(0, STEPS // 16, norm, 0)
    wk_copy.wait()
    wv_copy.wait()
    n_acc[...] = jnp.zeros_like(n_acc)
    q_acc[...] = jnp.zeros_like(q_acc)

    def project(k, carry):
        columns = pl.ds(pl.multiple_of(k * CHUNK, CHUNK), CHUNK)
        wq_copy(k).wait()
        rows = normed[:, columns]
        q_acc[...] += jnp.dot(rows, wq[columns, :], preferred_element_type=jnp.float32)
        n_acc[...] += lax.dot_general(rows, wkv[:, columns], NT, preferred_element_type=jnp.float32)
        return carry

    lax.fori_loop(0, CHUNKS, project, 0)

    mine = n_acc[...].astype(jnp.bfloat16)
    piece[...] = mine
    piece_copy = pltpu.make_async_remote_copy(
        src_ref=piece,
        dst_ref=other,
        send_sem=piece_sem.at[0],
        recv_sem=piece_sem.at[1],
        device_id=device(x, y + 1 - 2 * (y % 2), z, c),
        device_id_type=MESH,
    )
    piece_copy.start()
    for g in range(4):
        q_send[pl.ds(g * STEPS, STEPS), :] = q_acc[:, g * HD : (g + 1) * HD].astype(jnp.bfloat16)
    half = y % 2
    home_slot = 2 * (z // 2) + x // 2
    home_parity = (y // 2 + z // 2 + x // 2) % 2
    stays = half == home_parity

    def q_copy(i):
        bx, by, bz = i // 4, (i // 2) % 2, i % 2
        return pltpu.make_async_remote_copy(
            src_ref=q_send,
            dst_ref=q_buf.at[home_slot, half],
            send_sem=q_send_sem.at[i],
            recv_sem=q_recv_sem.at[home_slot, half],
            device_id=device((x + 2 * bx) % 4, home_parity + 2 * by, (z + 2 * bz) % 4, c),
            device_id_type=MESH,
        )

    def is_self(i):
        return (i // 4 == 0) & (i % 2 == 0) & (home_parity + 2 * ((i // 2) % 2) == y)

    def q_start(i, carry):
        @pl.when(jnp.logical_not(is_self(i)))
        def _():
            q_copy(i).start()

        @pl.when(is_self(i))
        def _():
            q_buf[home_slot, half] = q_send[...]

        return carry

    lax.fori_loop(0, SITES, q_start, 0)

    piece_copy.wait()
    mine = piece[...].astype(jnp.float32)
    theirs = other[...].astype(jnp.float32)
    low = jnp.where(half == 0, mine, theirs)
    high = jnp.where(half == 0, theirs, mine)
    first_half = lax.broadcasted_iota(jnp.int32, (STEPS, HD), 1) < 64
    new_keys = jnp.where(first_half, low, pltpu.roll(high, 64, 1)).astype(jnp.bfloat16)
    new_values = jnp.where(first_half, pltpu.roll(low, 64, 1), high).astype(jnp.bfloat16)
    ent_ref[pl.ds(0, STEPS), :] = new_keys
    ent_ref[pl.ds(STEPS, STEPS), :] = new_values
    scores = lax.dot_general(new_keys, q_send[...], NT, preferred_element_type=jnp.float32)
    key_step = lax.broadcasted_iota(jnp.int32, (STEPS, GROUP), 0)
    row_step = lax.broadcasted_iota(jnp.int32, (STEPS, GROUP), 1) % STEPS
    scores = jnp.where(key_step <= row_step, scores, LOWEST)
    top = jnp.max(scores, axis=0, keepdims=True)
    weights = jnp.exp2((scores - top) * EXP_SCALE)
    own_l[...] = jnp.broadcast_to(
        top * EXP_SCALE + jnp.log2(jnp.sum(weights, axis=0, keepdims=True)), (8, GROUP)
    )
    own_o[...] = lax.dot_general(
        new_values, weights.astype(jnp.bfloat16), TN, preferred_element_type=jnp.float32
    ) / jnp.sum(weights, axis=0, keepdims=True)

    key_row = lax.broadcasted_iota(jnp.int32, (KEYS, 2 * GROUP), 0)

    def home_of(t):
        u, v = t // 2, t % 2
        x0, z0 = 2 * v + x % 2, 2 * u + z % 2
        hlo = (y + u + v) % 2
        near = (x0 == x) & (z0 == z) & (hlo == y // 2)
        bx, bz = (x + 4 - x0) // 2 % 2, (z + 4 - z0) // 2 % 2
        return x0, z0, hlo, near, bx * 4 + (y // 2) * 2 + bz

    def out_copies(t, m):
        x0, z0, hlo, _, site = home_of(t)
        home = device(x0, 2 * hlo + m, z0, c)
        return (
            pltpu.make_async_remote_copy(
                src_ref=o_send.at[t, m],
                dst_ref=o_buf.at[site],
                send_sem=o_send_sem.at[t, m],
                recv_sem=o_recv_sem.at[site],
                device_id=home,
                device_id_type=MESH,
            ),
            pltpu.make_async_remote_copy(
                src_ref=l_send.at[t, m],
                dst_ref=l_buf.at[site],
                send_sem=l_send_sem.at[t, m],
                recv_sem=l_recv_sem.at[site],
                device_id=home,
                device_id_type=MESH,
            ),
        )

    def attend(t, carry):
        x0, z0, hlo, near, site = home_of(t)
        for m in range(2):

            @pl.when(jnp.logical_not(near & (y % 2 == m)))
            def _(m=m):
                pltpu.make_async_copy(
                    q_buf.at[t, m], q_buf.at[t, m], q_recv_sem.at[t, m]
                ).wait()

        arrived = recv.at[t, pl.ds(1, SOURCES - 1)]
        pltpu.make_async_copy(arrived, arrived, recv_sem.at[t]).wait()
        q = q_buf[t].reshape(2 * GROUP, HD)

        def score(i, top):
            s = lax.dot_general(recv[t, i, 0], q, NT, preferred_element_type=jnp.float32)
            s = jnp.where(key_row < live_keys[pl.ds(16 * t + i, 1), :], s, LOWEST)
            s_buf[pl.ds(pl.multiple_of(i * KEYS, KEYS), KEYS), :] = s
            return jnp.maximum(top, jnp.max(s.reshape(KEYS // 8, 8, 2 * GROUP), axis=0))

        top = lax.fori_loop(
            0, SOURCES, score, jnp.full((8, 2 * GROUP), LOWEST, jnp.float32)
        )
        top = jnp.max(top, axis=0, keepdims=True)

        def weigh(i, total):
            rows = pl.ds(pl.multiple_of(i * KEYS, KEYS), KEYS)
            w = jnp.exp2((s_buf[rows, :] - top) * EXP_SCALE)
            p_buf[rows, :] = w.astype(jnp.bfloat16)
            return total + jnp.sum(w.reshape(KEYS // 8, 8, 2 * GROUP), axis=0)

        total = lax.fori_loop(0, SOURCES, weigh, jnp.zeros((8, 2 * GROUP), jnp.float32))
        total = jnp.sum(total, axis=0, keepdims=True)
        values = recv[t, :, 1].reshape(SOURCES * KEYS, HD)
        o = lax.dot_general(values, p_buf[...], TN, preferred_element_type=jnp.float32)
        o = (o / total).astype(jnp.bfloat16)
        lse = jnp.broadcast_to(top * EXP_SCALE + jnp.log2(total), (8, 2 * GROUP))
        for m in range(2):
            o_send[t, m] = o[:, m * GROUP : (m + 1) * GROUP]
            l_send[t, m] = lse[:, m * GROUP : (m + 1) * GROUP]
            leaves = jnp.logical_not(near & (y % 2 == m))

            @pl.when(leaves)
            def _(m=m):
                for copy in out_copies(t, m):
                    copy.start()

            @pl.when(jnp.logical_not(leaves))
            def _(m=m):
                o_buf[site] = o_send[t, m]
                l_buf[site] = l_send[t, m]

        return carry

    lax.fori_loop(0, SLOTS, attend, 0)

    def await_site(i, carry):
        @pl.when(jnp.logical_not(is_self(i)))
        def _():
            pltpu.make_async_copy(o_buf.at[i], o_buf.at[i], o_recv_sem.at[i]).wait()
            pltpu.make_async_copy(l_buf.at[i], l_buf.at[i], l_recv_sem.at[i]).wait()

        return carry

    lax.fori_loop(0, SITES, await_site, 0)
    top = own_l[pl.ds(0, 1), :]
    for i in range(SITES):
        top = jnp.maximum(top, l_buf[i, pl.ds(0, 1), :])
    share = jnp.exp2(own_l[pl.ds(0, 1), :] - top)
    total = share
    result = own_o[...] * share
    for i in range(SITES):
        share = jnp.exp2(l_buf[i, pl.ds(0, 1), :] - top)
        total = total + share
        result = result + o_buf[i].astype(jnp.float32) * share
    result = (result / total).T
    for g in range(4):
        att_ref[:, g * HD : (g + 1) * HD] = result[g * STEPS : (g + 1) * STEPS, :].astype(
            jnp.bfloat16
        )

    pltpu.make_async_copy(packed, packed, pack_sem).wait()

    def await_q(i, carry):
        @pl.when(jnp.logical_not(is_self(i)))
        def _():
            q_copy(i).wait_send()

        return carry

    lax.fori_loop(0, SITES, await_q, 0)

    def await_out(t, carry):
        _, _, _, near, _ = home_of(t)
        for m in range(2):

            @pl.when(jnp.logical_not(near & (y % 2 == m)))
            def _(m=m):
                for copy in out_copies(t, m):
                    copy.wait_send()

        return carry

    lax.fori_loop(0, SLOTS, await_out, 0)


def per_device(
    new_tokens,
    norm_gain,
    query_weight,
    key_weight,
    value_weight,
    kv_cache,
    kept_blocks,
    kept_counts,
):
    vmem = pl.BlockSpec(memory_space=pltpu.VMEM)
    hbm = pl.BlockSpec(memory_space=pl.ANY)
    bf16, f32 = jnp.bfloat16, jnp.float32
    dma = pltpu.SemaphoreType.DMA
    attended, entries = pl.pallas_call(
        kernel,
        out_shape=(
            jax.ShapeDtypeStruct((STEPS, 4 * HD), bf16),
            jax.ShapeDtypeStruct((2 * STEPS, HD), bf16),
        ),
        in_specs=[hbm, vmem, hbm, hbm, hbm, hbm, vmem, vmem],
        out_specs=(vmem, vmem),
        scratch_shapes=[
            pltpu.VMEM((SLOTS, 2, 4, TOKD, 4 * HD), bf16),
            pltpu.VMEM((SLOTS * (SOURCES - 1), 2, KEYS, HD), bf16),
            pltpu.VMEM((SLOTS, SOURCES, 2, KEYS, HD), bf16),
            pltpu.VMEM((STEPS, WIDTH), bf16),
            pltpu.VMEM((STEPS, WIDTH), bf16),
            pltpu.VMEM((WIDTH, 4 * HD), bf16),
            pltpu.VMEM((HD, WIDTH), bf16),
            pltpu.VMEM((STEPS, 4 * HD), f32),
            pltpu.VMEM((STEPS, HD), f32),
            pltpu.VMEM((GROUP, HD), bf16),
            pltpu.VMEM((SLOTS, 2, GROUP, HD), bf16),
            pltpu.VMEM((CAP, 64, HD), jnp.int32),
            pltpu.VMEM((SLOTS * SOURCES, 2 * GROUP), jnp.int32),
            pltpu.VMEM((SOURCES * KEYS, 2 * GROUP), f32),
            pltpu.VMEM((SOURCES * KEYS, 2 * GROUP), bf16),
            pltpu.VMEM((SLOTS, 2, HD, GROUP), bf16),
            pltpu.VMEM((SLOTS, 2, 8, GROUP), f32),
            pltpu.VMEM((SITES, HD, GROUP), bf16),
            pltpu.VMEM((SITES, 8, GROUP), f32),
            pltpu.VMEM((HD, GROUP), f32),
            pltpu.VMEM((8, GROUP), f32),
            pltpu.VMEM((STEPS, HD), bf16),
            pltpu.VMEM((STEPS, HD), bf16),
            dma((SLOTS,)),
            dma((CHUNKS + 2,)),
            dma,
            dma,
            dma((SLOTS,)),
            dma((SITES,)),
            dma((SLOTS, 2)),
            dma((SLOTS, 2)),
            dma((SITES,)),
            dma((SLOTS, 2)),
            dma((SITES,)),
            dma((2,)),
        ],
        compiler_params=pltpu.CompilerParams(
            collective_id=0, has_side_effects=True, vmem_limit_bytes=56 * 1024 * 1024
        ),
    )(
        new_tokens.reshape(STEPS, WIDTH),
        norm_gain.reshape(1, WIDTH),
        query_weight,
        key_weight.T,
        value_weight.T,
        kv_cache,
        kept_blocks,
        kept_counts,
    )
    return (
        attended.reshape(STEPS, 1, 4 * HD),
        entries.reshape(1, 1, 2 * STEPS * HD),
    )


def solution(mesh):
    in_specs = (
        P(None, "seq", None),
        P(),
        P(None, "tp"),
        P(None, "tp"),
        P(None, "tp"),
        P(None, None, ("seq", "tp"), None),
        P(),
        P(),
    )
    out_specs = (P(None, "seq", "tp"), P("seq", "tp", None))
    return jax.shard_map(
        per_device, mesh=mesh, in_specs=in_specs, out_specs=out_specs, check_vma=False
    )
```

time: 179 us -> 75.1 us (0.42)
  the two profiles are of different devices: /device:TPU:1 before, /device:TPU:70 now
where the time goes in v1:
time: 75.1 us; the launch traced here: 74.8 us
  Pallas kernels  71.3 us (95%)
  local copies, waits for them, and re-layouts  2.88 us (4%)
    pallas_call x1, Pallas kernels, per_device(): pl.pallas_call(kernel, out_shape=(jax.ShapeDtypeStruct((STEPS, 4 * HD), b...  71.3 us

profile of v1, /device:TPU:70, one launch (start us, length us, event | category | flops | bytes accessed | tf_op | source)
XLA Modules:
  0.0 74.8 jit_solution(14622446199576202273)
XLA Ops:
  0.6 71.3 %shard_map.95 = (bf16[64,512]{1,0:T(8,128)(2,1)}, bf16[128,128]{1,0:T(8,128)(2,1)}) custom-call(bf16[64,8192]{1,0:T(8,128)(2,1)} %bitcast.5, f32[1,8192]{1,0:T(1,128)} %bitcast.9, bf16[8192,512]{1,0:T(8,128)(2,1)} %wq_hbm.1, bf16[64,8192]{1,0:T(8,128)(2,1)} %bitcast.6, bf16[64,8192]{1,0:T(8,128)(2,1)} %bitcast.7, bf16[2,8,256,1024]{3,2,1,0:T(8,128)(2,1)} %kv_hbm.1, ...), custom_call_target="tpu_custom_call" | custom-call | tf_op jit(solution)/shard_map/pallas_call | solution.py:473
  71.9 1.4 %reshape.19 = bf16[1,1,16384]{2,1,0:T(2,128)(2,1)} reshape(bf16[128,128]{1,0:T(8,128)(2,1)} %get-tuple-element.5) | data formatting | bytes 65536 | tf_op jit(solution)/shard_map/reshape | solution.py:533
  73.3 1.5 %copy.11 = bf16[64,1,512]{2,0,1:T(8,128)(2,1)} copy(bf16[64,1,512]{2,0,1:T(8,128)(2,1)} %bitcast.8) | data formatting | bytes 131072

commit v2 on v1

--- a/solution.py
+++ b/solution.py
@@ -52,8 +52,6 @@
     q_buf,
     pick,
     live_keys,
-    s_buf,
-    p_buf,
     o_send,
     l_send,
     o_buf,
@@ -84,22 +82,28 @@
     def device(x_, y_, z_, c_):
         return (z_ * 2 + c_, x_ * 4 + y_)
 
-    kv_copies = []
-    for t in range(SLOTS):
+    def kv_copy(t):
         u, v = t // 2, t % 2
-        kv_copies.append(
-            pltpu.make_async_copy(
-                kv_hbm.at[:, pl.ds(4 * u, 4), :, pl.ds(512 * v, 512)], kv_buf.at[t], kv_sem.at[t]
-            )
-        )
-        kv_copies[t].start()
+        return pltpu.make_async_copy(
+            kv_hbm.at[:, pl.ds(4 * u, 4), :, pl.ds(512 * v, 512)], kv_buf.at[t], kv_sem.at[t]
+        )
+
+    def wq_copy(k):
+        rows = pl.ds(pl.multiple_of(k * CHUNK, CHUNK), CHUNK)
+        return pltpu.make_async_copy(wq_hbm.at[rows], wq.at[rows], w_sem.at[k])
+
     tok_copy = pltpu.make_async_copy(tok_hbm, tok, tok_sem)
     wk_copy = pltpu.make_async_copy(wk_hbm, wkv.at[pl.ds(0, 64)], w_sem.at[CHUNKS])
     wv_copy = pltpu.make_async_copy(wv_hbm, wkv.at[pl.ds(64, 64)], w_sem.at[CHUNKS + 1])
-
-    def wq_copy(k):
-        rows = pl.ds(pl.multiple_of(k * CHUNK, CHUNK), CHUNK)
-        return pltpu.make_async_copy(wq_hbm.at[rows], wq.at[rows], w_sem.at[k])
+    kv_copy(0).start()
+    kv_copy(1).start()
+    tok_copy.start()
+    wk_copy.start()
+    wv_copy.start()
+    for k in range(CHUNKS):
+        wq_copy(k).start()
+    kv_copy(2).start()
+    kv_copy(3).start()
 
     barrier = pltpu.get_barrier_semaphore()
 
@@ -166,7 +170,6 @@
         live_keys[pl.ds(16 * t, 16), :] = jnp.broadcast_to(
             BLOCK * jnp.sum(here, axis=1, keepdims=True), (SOURCES, 2 * GROUP)
         )
-    pl.semaphore_wait(barrier, 68)
 
     def pack(t, cls, dst):
         u, v = t // 2, t % 2
@@ -190,21 +193,29 @@
             for kind in range(2):
                 dst[kind, pl.ds(slot * BLOCK, BLOCK), :] = part[kind]
 
-    for t in range(SLOTS):
+    def pack_slot(t):
+        kv_copy(t).wait()
+        pack(t, 0, recv.at[t, 0])
+
+        def one(cls, carry):
+            pack(t, cls, packed.at[t * 15 + cls - 1])
+            return carry
+
+        lax.fori_loop(1, SOURCES, one, 0)
+
+    def send_slot(t):
         u, v = t // 2, t % 2
-        kv_copies[t].wait()
-
-        def send(cls, carry, t=t, u=u, v=v):
+
+        def one(i, carry):
+            cls = (i * 5) % 16
             dx, dy, dz, dc = cls // 8, (cls // 4) % 2, (cls // 2) % 2, cls % 2
             rx, ry, rz, rc = (x + dx) % 2, (y + dy) % 2, (z + dz) % 2, (c + dc) % 2
             ax, ay, az = (u + ry) % 2, (v + rz) % 2, (u + v + rx) % 2
             x_ = (x + dx * (1 - 2 * ((x + ax) % 2)) + 4) % 4
             y_ = (y + dy * (1 - 2 * ((y + ay) % 2)) + 4) % 4
             z_ = (z + dz * (1 - 2 * ((z + az) % 2)) + 4) % 4
-            place = t * 15 + cls - 1
-            pack(t, cls, packed.at[place])
             pltpu.make_async_remote_copy(
-                src_ref=packed.at[place],
+                src_ref=packed.at[t * 15 + cls - 1],
                 dst_ref=recv.at[t, cls],
                 send_sem=pack_sem,
                 recv_sem=recv_sem.at[t],
@@ -213,15 +224,13 @@
             ).start()
             return carry
 
-        lax.fori_loop(1, SOURCES, send, 0)
-        if t == 0:
-            tok_copy.start()
-            wk_copy.start()
-            wv_copy.start()
-            for k in range(CHUNKS):
-                wq_copy(k).start()
-    for t in range(SLOTS):
-        pack(t, 0, recv.at[t, 0])
+        lax.fori_loop(1, SOURCES, one, 0)
+
+    pack_slot(0)
+    pl.semaphore_wait(barrier, 68)
+    send_slot(0)
+    pack_slot(1)
+    send_slot(1)
 
     tok_copy.wait()
 
@@ -294,6 +303,10 @@
         return carry
 
     lax.fori_loop(0, SITES, q_start, 0)
+
+    for t in range(2, SLOTS):
+        pack_slot(t)
+        send_slot(t)
 
     piece_copy.wait()
     mine = piece[...].astype(jnp.float32)
@@ -364,27 +377,26 @@
         pltpu.make_async_copy(arrived, arrived, recv_sem.at[t]).wait()
         q = q_buf[t].reshape(2 * GROUP, HD)
 
-        def score(i, top):
-            s = lax.dot_general(recv[t, i, 0], q, NT, preferred_element_type=jnp.float32)
-            s = jnp.where(key_row < live_keys[pl.ds(16 * t + i, 1), :], s, LOWEST)
-            s_buf[pl.ds(pl.multiple_of(i * KEYS, KEYS), KEYS), :] = s
-            return jnp.maximum(top, jnp.max(s.reshape(KEYS // 8, 8, 2 * GROUP), axis=0))
-
-        top = lax.fori_loop(
-            0, SOURCES, score, jnp.full((8, 2 * GROUP), LOWEST, jnp.float32)
-        )
-        top = jnp.max(top, axis=0, keepdims=True)
-
-        def weigh(i, total):
-            rows = pl.ds(pl.multiple_of(i * KEYS, KEYS), KEYS)
-            w = jnp.exp2((s_buf[rows, :] - top) * EXP_SCALE)
-            p_buf[rows, :] = w.astype(jnp.bfloat16)
-            return total + jnp.sum(w.reshape(KEYS // 8, 8, 2 * GROUP), axis=0)
-
-        total = lax.fori_loop(0, SOURCES, weigh, jnp.zeros((8, 2 * GROUP), jnp.float32))
-        total = jnp.sum(total, axis=0, keepdims=True)
+        keys = recv[t, :, 0].reshape(SOURCES * KEYS, HD)
         values = recv[t, :, 1].reshape(SOURCES * KEYS, HD)
-        o = lax.dot_general(values, p_buf[...], TN, preferred_element_type=jnp.float32)
+        s = lax.dot_general(keys, q, NT, preferred_element_type=jnp.float32)
+        s = jnp.concatenate(
+            [
+                jnp.where(
+                    key_row < live_keys[pl.ds(16 * t + i, 1), :],
+                    s[i * KEYS : (i + 1) * KEYS],
+                    LOWEST,
+                )
+                for i in range(SOURCES)
+            ],
+            axis=0,
+        )
+        top = jnp.max(s, axis=0, keepdims=True)
+        w = jnp.exp2((s - top) * EXP_SCALE)
+        total = jnp.sum(w, axis=0, keepdims=True)
+        o = lax.dot_general(
+            values, w.astype(jnp.bfloat16), TN, preferred_element_type=jnp.float32
+        )
         o = (o / total).astype(jnp.bfloat16)
         lse = jnp.broadcast_to(top * EXP_SCALE + jnp.log2(total), (8, 2 * GROUP))
         for m in range(2):
@@ -492,8 +504,6 @@
             pltpu.VMEM((SLOTS, 2, GROUP, HD), bf16),
             pltpu.VMEM((CAP, 64, HD), jnp.int32),
             pltpu.VMEM((SLOTS * SOURCES, 2 * GROUP), jnp.int32),
-            pltpu.VMEM((SOURCES * KEYS, 2 * GROUP), f32),
-            pltpu.VMEM((SOURCES * KEYS, 2 * GROUP), bf16),
             pltpu.VMEM((SLOTS, 2, HD, GROUP), bf16),
             pltpu.VMEM((SLOTS, 2, 8, GROUP), f32),
             pltpu.VMEM((SITES, HD, GROUP), bf16),

time: 75.1 us -> 63.4 us (0.84)
  the two profiles are of different devices: /device:TPU:70 before, /device:TPU:1 now
where the time goes in v2:
time: 63.4 us; the launch traced here: 63.1 us
  Pallas kernels  59.6 us (94%)
  local copies, waits for them, and re-layouts  2.88 us (5%)
  between operations  0.64 us (1%)
    pallas_call x1, Pallas kernels, per_device(): pl.pallas_call(kernel, out_shape=(jax.ShapeDtypeStruct((STEPS, 4 * HD), b...  59.6 us
    unnamed x1, local copies, waits for them, and re-layouts  1.47 us
    reshape x1, local copies, waits for them, and re-layouts, per_device(): entries.reshape(1, 1, 2 * STEPS * HD)  1.4 us

profile of v2, /device:TPU:1, one launch (start us, length us, event | category | flops | bytes accessed | tf_op | source)
XLA Modules:
  0.0 63.1 jit_solution(2923635701614898019)
XLA Ops:
  0.6 59.6 %shard_map.95 = (bf16[64,512]{1,0:T(8,128)(2,1)}, bf16[128,128]{1,0:T(8,128)(2,1)}) custom-call(bf16[64,8192]{1,0:T(8,128)(2,1)} %bitcast.5, f32[1,8192]{1,0:T(1,128)} %bitcast.9, bf16[8192,512]{1,0:T(8,128)(2,1)} %wq_hbm.1, bf16[64,8192]{1,0:T(8,128)(2,1)} %bitcast.6, bf16[64,8192]{1,0:T(8,128)(2,1)} %bitcast.7, bf16[2,8,256,1024]{3,2,1,0:T(8,128)(2,1)} %kv_hbm.1, ...), custom_call_target="tpu_custom_call" | custom-call | tf_op jit(solution)/shard_map/pallas_call | solution.py:485
  60.3 1.4 %reshape.19 = bf16[1,1,16384]{2,1,0:T(2,128)(2,1)} reshape(bf16[128,128]{1,0:T(8,128)(2,1)} %get-tuple-element.5) | data formatting | bytes 65536 | tf_op jit(solution)/shard_map/reshape | solution.py:543
  61.7 1.5 %copy.11 = bf16[64,1,512]{2,0,1:T(8,128)(2,1)} copy(bf16[64,1,512]{2,0,1:T(8,128)(2,1)} %bitcast.8) | data formatting | bytes 131072

commit v3 on v2

--- a/solution.py
+++ b/solution.py
@@ -30,15 +30,18 @@
 
 def kernel(
     tok_hbm,
-    gain_ref,
+    gain_hbm,
     wq_hbm,
     wk_hbm,
     wv_hbm,
     kv_hbm,
+    kept_hbm,
+    counts_hbm,
+    att_ref,
+    ent_ref,
+    gain_ref,
     kept_ref,
     counts_ref,
-    att_ref,
-    ent_ref,
     kv_buf,
     packed,
     recv,
@@ -63,6 +66,7 @@
     kv_sem,
     w_sem,
     tok_sem,
+    small_sem,
     pack_sem,
     recv_sem,
     q_send_sem,
@@ -82,11 +86,28 @@
     def device(x_, y_, z_, c_):
         return (z_ * 2 + c_, x_ * 4 + y_)
 
-    def kv_copy(t):
+    def other_y(y_, odd):
+        return (y_ + 1 - 2 * ((y_ + 1 + odd) % 2) + 4) % 4
+
+    def pair_at(x_, y_, z_, c_, u, v):
+        g = 1 - 2 * c_
+        x0, z0 = (x_ - v * g + 4) % 4, (z_ - u * g + 4) % 4
+        row = (y_ + ((x0 + z0) % 2) * (1 + 2 * c_)) % 4
+        return x0, z0, row // 2, row % 2
+
+    def kv_start(t):
         u, v = t // 2, t % 2
-        return pltpu.make_async_copy(
-            kv_hbm.at[:, pl.ds(4 * u, 4), :, pl.ds(512 * v, 512)], kv_buf.at[t], kv_sem.at[t]
-        )
+        for part in range(8):
+            dc, dz, dx = part // 4, (part // 2) % 2, part % 2
+            c_ = (c + dc) % 2
+            g = 1 - 2 * c_
+            x0 = (x - dx * g * (2 * v - 1) - v * g + 8) % 4
+            z0 = (z - dz * g * (2 * u - 1) - u * g + 8) % 4
+            pltpu.make_async_copy(
+                kv_hbm.at[:, 2 * z0 + c_, :, pl.ds(pl.multiple_of(x0 * 2 * HD, 2 * HD), 2 * HD)],
+                kv_buf.at[t, part],
+                kv_sem.at[t],
+            ).start()
 
     def wq_copy(k):
         rows = pl.ds(pl.multiple_of(k * CHUNK, CHUNK), CHUNK)
@@ -95,15 +116,14 @@
     tok_copy = pltpu.make_async_copy(tok_hbm, tok, tok_sem)
     wk_copy = pltpu.make_async_copy(wk_hbm, wkv.at[pl.ds(0, 64)], w_sem.at[CHUNKS])
     wv_copy = pltpu.make_async_copy(wv_hbm, wkv.at[pl.ds(64, 64)], w_sem.at[CHUNKS + 1])
-    kv_copy(0).start()
-    kv_copy(1).start()
-    tok_copy.start()
-    wk_copy.start()
-    wv_copy.start()
-    for k in range(CHUNKS):
-        wq_copy(k).start()
-    kv_copy(2).start()
-    kv_copy(3).start()
+    gain_copy = pltpu.make_async_copy(gain_hbm, gain_ref, small_sem.at[0])
+    kept_copy = pltpu.make_async_copy(kept_hbm, kept_ref, small_sem.at[1])
+    counts_copy = pltpu.make_async_copy(counts_hbm, counts_ref, small_sem.at[2])
+    kept_copy.start()
+    counts_copy.start()
+    kv_start(3)
+    kv_start(2)
+    gain_copy.start()
 
     barrier = pltpu.get_barrier_semaphore()
 
@@ -124,14 +144,17 @@
     lax.fori_loop(0, 54, greet_near, 0)
 
     def greet_far(i, carry):
-        y_ = (y + i % 4) % 4
-        z_ = (z + 2 * ((i // 4) % 2)) % 4
-        x_ = (x + 2 * (i // 8)) % 4
-        pl.semaphore_signal(barrier, inc=1, device_id=device(x_, y_, z_, c), device_id_type=MESH)
-        return carry
-
-    lax.fori_loop(1, 16, greet_far, 0)
-
+        z_ = (z + i % 3 + 3) % 4
+        x_ = (x + i // 3 + 3) % 4
+        pl.semaphore_signal(
+            barrier, inc=1, device_id=device(x_, (y + 2) % 4, z_, c), device_id_type=MESH
+        )
+        return carry
+
+    lax.fori_loop(0, 9, greet_far, 0)
+
+    kept_copy.wait()
+    counts_copy.wait()
     lane = lax.broadcasted_iota(jnp.int32, (8, 256), 1)
     eye = lax.broadcasted_iota(jnp.int32, (8, 8), 0) == lax.broadcasted_iota(jnp.int32, (8, 8), 1)
     lane_8 = lax.broadcasted_iota(jnp.int32, (1, 8), 1)
@@ -152,17 +175,17 @@
     sz, sc = (source >> 1) & 1, source & 1
     for t in range(SLOTS):
         u, v = t // 2, t % 2
-        ax, ay, az = (u + y) % 2, (v + z) % 2, (u + v + x) % 2
-        nx = (x + 5 - 2 * ((x + ax) % 2)) % 4
-        ny = (y + 5 - 2 * ((y + ay) % 2)) % 4
-        nz = (z + 5 - 2 * ((z + az) % 2)) % 4
+        g = 1 - 2 * c
+        x0, z0, hlo, _ = pair_at(x, y, z, c, u, v)
+        nx = (x + g * (2 * v - 1) + 4) % 4
+        nz = (z + g * (2 * u - 1) + 4) % 4
+        ny = other_y(y, (x0 + z0) % 2)
         fx = jnp.where(sx == 0, x, nx)
         fy = jnp.where(sy == 0, y, ny)
         fz = jnp.where(sz == 0, z, nz)
         fc = jnp.where(sc == 0, c, 1 - c)
         owner = (fz * 2 + fc) * 16 + fx * 4 + fy
-        p_ = 2 * (2 * u + z % 2) + c
-        h_ = 2 * (2 * v + x % 2) + (y + u + v) % 2
+        p_, h_ = 2 * z0 + c, 2 * x0 + hlo
         row = kept_ref[p_, pl.ds(h_, 1), :]
         counts = jnp.where(lane_8 == h_, counts_ref[pl.ds(p_, 1), :], 0)
         live = lane_16 < jnp.sum(counts, axis=1, keepdims=True)
@@ -171,31 +194,36 @@
             BLOCK * jnp.sum(here, axis=1, keepdims=True), (SOURCES, 2 * GROUP)
         )
 
+    def site_of(t, cls):
+        u, v = t // 2, t % 2
+        dx, dy, dz, c_ = cls // 8, (cls // 4) % 2, (cls // 2) % 2, (c + cls) % 2
+        g = 1 - 2 * c_
+        x_ = (x - dx * g * (2 * v - 1) + 4) % 4
+        z_ = (z - dz * g * (2 * u - 1) + 4) % 4
+        odd = (x_ + z_ + u + v) % 2
+        y_ = y + dy * (other_y(y, odd) - y)
+        return x_, y_, z_, c_
+
     def pack(t, cls, dst):
-        u, v = t // 2, t % 2
-        rx = (x + cls // 8) % 2
-        ry = (y + cls // 4) % 2
-        rz = (z + cls // 2) % 2
-        rc = (c + cls) % 2
-        p_loc = 2 * rz + rc
-        h_loc = 2 * rx + (ry + u + v) % 2
-        pair = (4 * u + p_loc) * 8 + 4 * v + h_loc
-        columns = pl.ds(pl.multiple_of(h_loc * HD, HD), HD)
+        x_, y_, z_, c_ = site_of(t, cls)
+        x0, z0, hlo, _ = pair_at(x_, y_, z_, c_, t // 2, t % 2)
+        part = (cls % 2) * 4 + ((cls // 2) % 2) * 2 + cls // 8
+        pair = (2 * z0 + c_) * 8 + 2 * x0 + hlo
+        columns = pl.ds(pl.multiple_of(hlo * HD, HD), HD)
         for slot in range(CAP):
             chosen = jnp.broadcast_to(pick[slot, pl.ds(pair, 1), :], (16, HD))
-            part = [None, None]
+            total = [None, None]
             for block in range(slot, 4):
                 weight = jnp.where(chosen == block, 1.0, 0.0).astype(jnp.bfloat16)
                 weight = jnp.concatenate([weight] * (BLOCK // 16), axis=0)
                 for kind in range(2):
-                    rows = kv_buf[t, kind, p_loc, pl.ds(block * BLOCK, BLOCK), columns] * weight
-                    part[kind] = rows if part[kind] is None else part[kind] + rows
+                    rows = kv_buf[t, part, kind, pl.ds(block * BLOCK, BLOCK), columns] * weight
+                    total[kind] = rows if total[kind] is None else total[kind] + rows
             for kind in range(2):
-                dst[kind, pl.ds(slot * BLOCK, BLOCK), :] = part[kind]
+                dst[kind, pl.ds(slot * BLOCK, BLOCK), :] = total[kind]
 
     def pack_slot(t):
-        kv_copy(t).wait()
-        pack(t, 0, recv.at[t, 0])
+        pltpu.make_async_copy(kv_buf.at[t], kv_buf.at[t], kv_sem.at[t]).wait()
 
         def one(cls, carry):
             pack(t, cls, packed.at[t * 15 + cls - 1])
@@ -204,35 +232,35 @@
         lax.fori_loop(1, SOURCES, one, 0)
 
     def send_slot(t):
-        u, v = t // 2, t % 2
-
         def one(i, carry):
             cls = (i * 5) % 16
-            dx, dy, dz, dc = cls // 8, (cls // 4) % 2, (cls // 2) % 2, cls % 2
-            rx, ry, rz, rc = (x + dx) % 2, (y + dy) % 2, (z + dz) % 2, (c + dc) % 2
-            ax, ay, az = (u + ry) % 2, (v + rz) % 2, (u + v + rx) % 2
-            x_ = (x + dx * (1 - 2 * ((x + ax) % 2)) + 4) % 4
-            y_ = (y + dy * (1 - 2 * ((y + ay) % 2)) + 4) % 4
-            z_ = (z + dz * (1 - 2 * ((z + az) % 2)) + 4) % 4
             pltpu.make_async_remote_copy(
                 src_ref=packed.at[t * 15 + cls - 1],
                 dst_ref=recv.at[t, cls],
                 send_sem=pack_sem,
                 recv_sem=recv_sem.at[t],
-                device_id=device(x_, y_, z_, rc),
+                device_id=device(*site_of(t, cls)),
                 device_id_type=MESH,
             ).start()
             return carry
 
         lax.fori_loop(1, SOURCES, one, 0)
 
-    pack_slot(0)
-    pl.semaphore_wait(barrier, 68)
-    send_slot(0)
-    pack_slot(1)
-    send_slot(1)
+    pack_slot(3)
+    pl.semaphore_wait(barrier, 62)
+    send_slot(3)
+    tok_copy.start()
+    wk_copy.start()
+    wv_copy.start()
+    for k in range(CHUNKS):
+        wq_copy(k).start()
+    kv_start(1)
+    kv_start(0)
+    pack_slot(2)
+    send_slot(2)
 
     tok_copy.wait()
+    gain_copy.wait()
 
     def norm(i, carry):
         rows = pl.ds(pl.multiple_of(i * 16, 16), 16)
@@ -273,23 +301,27 @@
     for g in range(4):
         q_send[pl.ds(g * STEPS, STEPS), :] = q_acc[:, g * HD : (g + 1) * HD].astype(jnp.bfloat16)
     half = y % 2
-    home_slot = 2 * (z // 2) + x // 2
-    home_parity = (y // 2 + z // 2 + x // 2) % 2
-    stays = half == home_parity
+    toward = 1 - 2 * c
+    shift = ((x + z) % 2) * (1 + 2 * c)
+
+    def site_y(i):
+        return (2 * (y // 2) + (i // 2) % 2 - shift + 4) % 4
 
     def q_copy(i):
-        bx, by, bz = i // 4, (i // 2) % 2, i % 2
+        bx, bz = i // 4, i % 2
         return pltpu.make_async_remote_copy(
             src_ref=q_send,
-            dst_ref=q_buf.at[home_slot, half],
+            dst_ref=q_buf.at[2 * bz + bx, half],
             send_sem=q_send_sem.at[i],
-            recv_sem=q_recv_sem.at[home_slot, half],
-            device_id=device((x + 2 * bx) % 4, home_parity + 2 * by, (z + 2 * bz) % 4, c),
+            recv_sem=q_recv_sem.at[2 * bz + bx, half],
+            device_id=device(
+                (x + bx * toward + 4) % 4, site_y(i), (z + bz * toward + 4) % 4, c
+            ),
             device_id_type=MESH,
         )
 
     def is_self(i):
-        return (i // 4 == 0) & (i % 2 == 0) & (home_parity + 2 * ((i // 2) % 2) == y)
+        return (i // 4 == 0) & (i % 2 == 0) & (site_y(i) == y)
 
     def q_start(i, carry):
         @pl.when(jnp.logical_not(is_self(i)))
@@ -298,13 +330,13 @@
 
         @pl.when(is_self(i))
         def _():
-            q_buf[home_slot, half] = q_send[...]
+            q_buf[0, half] = q_send[...]
 
         return carry
 
     lax.fori_loop(0, SITES, q_start, 0)
 
-    for t in range(2, SLOTS):
+    for t in (1, 0):
         pack_slot(t)
         send_slot(t)
 
@@ -335,11 +367,9 @@
 
     def home_of(t):
         u, v = t // 2, t % 2
-        x0, z0 = 2 * v + x % 2, 2 * u + z % 2
-        hlo = (y + u + v) % 2
-        near = (x0 == x) & (z0 == z) & (hlo == y // 2)
-        bx, bz = (x + 4 - x0) // 2 % 2, (z + 4 - z0) // 2 % 2
-        return x0, z0, hlo, near, bx * 4 + (y // 2) * 2 + bz
+        x0, z0, hlo, by = pair_at(x, y, z, c, u, v)
+        near = (t == 0) & (hlo == y // 2)
+        return x0, z0, hlo, near, v * 4 + by * 2 + u
 
     def out_copies(t, m):
         x0, z0, hlo, _, site = home_of(t)
@@ -363,7 +393,8 @@
             ),
         )
 
-    def attend(t, carry):
+    def attend(step, carry):
+        t = SLOTS - 1 - step
         x0, z0, hlo, near, site = home_of(t)
         for m in range(2):
 
@@ -375,6 +406,7 @@
 
         arrived = recv.at[t, pl.ds(1, SOURCES - 1)]
         pltpu.make_async_copy(arrived, arrived, recv_sem.at[t]).wait()
+        pack(t, 0, recv.at[t, 0])
         q = q_buf[t].reshape(2 * GROUP, HD)
 
         keys = recv[t, :, 0].reshape(SOURCES * KEYS, HD)
@@ -466,6 +498,12 @@
         return carry
 
     lax.fori_loop(0, SLOTS, await_out, 0)
+
+
+def place(att_ref, ent_ref, att_out, ent_out):
+    att_out[...] = att_ref[...]
+    for row in range(2 * STEPS):
+        ent_out[0, :, row * HD : (row + 1) * HD] = ent_ref[row : row + 1, :]
 
 
 def per_device(
@@ -488,10 +526,13 @@
             jax.ShapeDtypeStruct((STEPS, 4 * HD), bf16),
             jax.ShapeDtypeStruct((2 * STEPS, HD), bf16),
         ),
-        in_specs=[hbm, vmem, hbm, hbm, hbm, hbm, vmem, vmem],
+        in_specs=[hbm] * 8,
         out_specs=(vmem, vmem),
         scratch_shapes=[
-            pltpu.VMEM((SLOTS, 2, 4, TOKD, 4 * HD), bf16),
+            pltpu.VMEM((1, WIDTH), f32),
+            pltpu.VMEM((8, 8, 256), jnp.int32),
+            pltpu.VMEM((8, 8), jnp.int32),
+            pltpu.VMEM((SLOTS, 8, 2, TOKD, 2 * HD), bf16),
             pltpu.VMEM((SLOTS * (SOURCES - 1), 2, KEYS, HD), bf16),
             pltpu.VMEM((SLOTS, SOURCES, 2, KEYS, HD), bf16),
             pltpu.VMEM((STEPS, WIDTH), bf16),
@@ -515,6 +556,7 @@
             dma((SLOTS,)),
             dma((CHUNKS + 2,)),
             dma,
+            dma((3,)),
             dma,
             dma((SLOTS,)),
             dma((SITES,)),
@@ -538,10 +580,16 @@
         kept_blocks,
         kept_counts,
     )
-    return (
-        attended.reshape(STEPS, 1, 4 * HD),
-        entries.reshape(1, 1, 2 * STEPS * HD),
-    )
+    attended, entries = pl.pallas_call(
+        place,
+        out_shape=(
+            jax.ShapeDtypeStruct((STEPS, 4 * HD), bf16),
+            jax.ShapeDtypeStruct((1, 1, 2 * STEPS * HD), bf16),
+        ),
+        in_specs=[vmem, vmem],
+        out_specs=(vmem, vmem),
+    )(attended, entries)
+    return attended.reshape(STEPS, 1, 4 * HD), entries
 
 
 def solution(mesh):

time: 63.4 us -> 54 us (0.85)
  Pallas kernels: 59.6 us -> 52.9 us
  local copies, waits for them, and re-layouts: 2.88 us -> 0 us
    pallas_call x1, Pallas kernels: 59.6 us -> 51.3 us  [per_device(): pl.pallas_call(kernel, out_shape=(jax.ShapeDtypeStruct((STEPS, 4 * HD), b...]
    pallas_call x0 -> x1, Pallas kernels: none -> 1.58 us  [per_device(): pl.pallas_call(place, out_shape=(jax.ShapeDtypeStruct((STEPS, 4 * HD), bf...]
    unnamed x1 -> x0, local copies, waits for them, and re-layouts: 1.47 us -> none
    reshape x1 -> x0, local copies, waits for them, and re-layouts: 1.4 us -> none  [per_device(): entries.reshape(1, 1, 2 * STEPS * HD)]
where the time goes in v3:
time: 54 us; the launch traced here: 53.5 us
  Pallas kernels  52.9 us (98%)
  between operations  0.64 us (1%)
    pallas_call x1, Pallas kernels, per_device(): pl.pallas_call(kernel, out_shape=(jax.ShapeDtypeStruct((STEPS, 4 * HD), b...  51.3 us
    pallas_call x1, Pallas kernels, per_device(): pl.pallas_call(place, out_shape=(jax.ShapeDtypeStruct((STEPS, 4 * HD), bf...  1.58 us

profile of v3, /device:TPU:1, one launch (start us, length us, event | category | flops | bytes accessed | tf_op | source)
XLA Modules:
  0.0 53.5 jit_solution(17313260863309754138)
XLA Ops:
  0.6 51.3 %shard_map.95 = (bf16[64,512]{1,0:T(8,128)(2,1)}, bf16[128,128]{1,0:T(8,128)(2,1)}) custom-call(bf16[64,8192]{1,0:T(8,128)(2,1)} %bitcast.5, f32[1,8192]{1,0:T(1,128)} %bitcast.8, bf16[8192,512]{1,0:T(8,128)(2,1)} %wq_hbm.1, bf16[64,8192]{1,0:T(8,128)(2,1)} %bitcast.6, bf16[64,8192]{1,0:T(8,128)(2,1)} %bitcast.7, bf16[2,8,256,1024]{3,2,1,0:T(8,128)(2,1)} %kv_hbm.1, ...), custom_call_target="tpu_custom_call" | custom-call | tf_op jit(solution)/shard_map/pallas_call | solution.py:523
  51.9 1.6 %shard_map.96 = (bf16[64,512]{1,0:T(8,128)(2,1)}, bf16[1,1,16384]{2,1,0:T(2,128)(2,1)}) custom-call(bf16[64,512]{1,0:T(8,128)(2,1)} %get-tuple-element.6.att_ref, bf16[128,128]{1,0:T(8,128)(2,1)} %get-tuple-element.7.ent_ref), custom_call_target="tpu_custom_call" | custom-call | tf_op jit(solution)/shard_map/pallas_call | solution.py:583

commit v4 on v3

--- a/solution.py
+++ b/solution.py
@@ -89,10 +89,14 @@
     def other_y(y_, odd):
         return (y_ + 1 - 2 * ((y_ + 1 + odd) % 2) + 4) % 4
 
+    def odd_of(x0, z0, c_):
+        more = (1 - c_) * (1 - x0 % 2) * (1 - ((z0 - x0 + 4) % 4) // 2)
+        return ((x0 + z0) % 2) * (1 - more)
+
     def pair_at(x_, y_, z_, c_, u, v):
         g = 1 - 2 * c_
         x0, z0 = (x_ - v * g + 4) % 4, (z_ - u * g + 4) % 4
-        row = (y_ + ((x0 + z0) % 2) * (1 + 2 * c_)) % 4
+        row = (y_ + odd_of(x0, z0, c_) * (1 + 2 * c_)) % 4
         return x0, z0, row // 2, row % 2
 
     def kv_start(t):
@@ -126,32 +130,20 @@
     gain_copy.start()
 
     barrier = pltpu.get_barrier_semaphore()
-
-    def greet_near(i, carry):
-        c_ = (c + i) % 2
-        z_ = (z + (i // 2) % 3 + 3) % 4
-        y_ = (y + (i // 6) % 3 + 3) % 4
-        x_ = (x + i // 18 + 3) % 4
-
-        @pl.when(i != 26)
-        def _():
-            pl.semaphore_signal(
-                barrier, inc=1, device_id=device(x_, y_, z_, c_), device_id_type=MESH
-            )
-
-        return carry
-
-    lax.fori_loop(0, 54, greet_near, 0)
-
-    def greet_far(i, carry):
-        z_ = (z + i % 3 + 3) % 4
-        x_ = (x + i // 3 + 3) % 4
-        pl.semaphore_signal(
-            barrier, inc=1, device_id=device(x_, (y + 2) % 4, z_, c), device_id_type=MESH
-        )
-        return carry
-
-    lax.fori_loop(0, 9, greet_far, 0)
+    xs = [x, (x + 1) % 4, (x + 3) % 4]
+    ys = [y, (y + 1) % 4, (y + 3) % 4, (y + 2) % 4]
+    zs = [z, (z + 1) % 4, (z + 3) % 4]
+    for i in range(3):
+        for j in range(4):
+            for k in range(3):
+                for c_ in (c, 1 - c)[: 1 if j == 3 else 2]:
+                    if i or j or k or c_ is not c:
+                        pl.semaphore_signal(
+                            barrier,
+                            inc=1,
+                            device_id=device(xs[i], ys[j], zs[k], c_),
+                            device_id_type=MESH,
+                        )
 
     kept_copy.wait()
     counts_copy.wait()
@@ -179,7 +171,7 @@
         x0, z0, hlo, _ = pair_at(x, y, z, c, u, v)
         nx = (x + g * (2 * v - 1) + 4) % 4
         nz = (z + g * (2 * u - 1) + 4) % 4
-        ny = other_y(y, (x0 + z0) % 2)
+        ny = other_y(y, odd_of(x0, z0, c))
         fx = jnp.where(sx == 0, x, nx)
         fy = jnp.where(sy == 0, y, ny)
         fz = jnp.where(sz == 0, z, nz)
@@ -200,7 +192,7 @@
         g = 1 - 2 * c_
         x_ = (x - dx * g * (2 * v - 1) + 4) % 4
         z_ = (z - dz * g * (2 * u - 1) + 4) % 4
-        odd = (x_ + z_ + u + v) % 2
+        odd = odd_of((x_ - v * g + 4) % 4, (z_ - u * g + 4) % 4, c_)
         y_ = y + dy * (other_y(y, odd) - y)
         return x_, y_, z_, c_
 
@@ -302,7 +294,7 @@
         q_send[pl.ds(g * STEPS, STEPS), :] = q_acc[:, g * HD : (g + 1) * HD].astype(jnp.bfloat16)
     half = y % 2
     toward = 1 - 2 * c
-    shift = ((x + z) % 2) * (1 + 2 * c)
+    shift = odd_of(x, z, c) * (1 + 2 * c)
 
     def site_y(i):
         return (2 * (y // 2) + (i // 2) % 2 - shift + 4) % 4

time: 54 us -> 50.9 us (0.943)
  Pallas kernels: 52.9 us -> 49.4 us
    pallas_call x1, Pallas kernels: 51.3 us -> 47.8 us  [per_device(): pl.pallas_call(kernel, out_shape=(jax.ShapeDtypeStruct((STEPS, 4 * HD), b...]
where the time goes in v4:
time: 50.9 us; the launch traced here: 50.1 us
  Pallas kernels  49.4 us (97%)
  between operations  0.64 us (1%)
    pallas_call x1, Pallas kernels, per_device(): pl.pallas_call(kernel, out_shape=(jax.ShapeDtypeStruct((STEPS, 4 * HD), b...  47.8 us
    pallas_call x1, Pallas kernels, per_device(): pl.pallas_call(place, out_shape=(jax.ShapeDtypeStruct((STEPS, 4 * HD), bf...  1.58 us

profile of v4, /device:TPU:1, one launch (start us, length us, event | category | flops | bytes accessed | tf_op | source)
XLA Modules:
  0.0 50.1 jit_solution(17553585726964301066)
XLA Ops:
  0.6 47.8 %shard_map.95 = (bf16[64,512]{1,0:T(8,128)(2,1)}, bf16[128,128]{1,0:T(8,128)(2,1)}) custom-call(bf16[64,8192]{1,0:T(8,128)(2,1)} %bitcast.5, f32[1,8192]{1,0:T(1,128)} %bitcast.8, bf16[8192,512]{1,0:T(8,128)(2,1)} %wq_hbm.1, bf16[64,8192]{1,0:T(8,128)(2,1)} %bitcast.6, bf16[64,8192]{1,0:T(8,128)(2,1)} %bitcast.7, bf16[2,8,256,1024]{3,2,1,0:T(8,128)(2,1)} %kv_hbm.1, ...), custom_call_target="tpu_custom_call" | custom-call | tf_op jit(solution)/shard_map/pallas_call | solution.py:515
  48.5 1.6 %shard_map.96 = (bf16[64,512]{1,0:T(8,128)(2,1)}, bf16[1,1,16384]{2,1,0:T(2,128)(2,1)}) custom-call(bf16[64,512]{1,0:T(8,128)(2,1)} %get-tuple-element.6.att_ref, bf16[128,128]{1,0:T(8,128)(2,1)} %get-tuple-element.7.ent_ref), custom_call_target="tpu_custom_call" | custom-call | tf_op jit(solution)/shard_map/pallas_call | solution.py:575

commit v5 on v4

--- a/solution.py
+++ b/solution.py
@@ -225,7 +225,7 @@
 
     def send_slot(t):
         def one(i, carry):
-            cls = (i * 5) % 16
+            cls = (i * (5 + 2 * c)) % 16
             pltpu.make_async_remote_copy(
                 src_ref=packed.at[t * 15 + cls - 1],
                 dst_ref=recv.at[t, cls],

time: 50.9 us -> 50.7 us (level)
  no operation moved by 1% of the time
where the time goes in v5:
time: 50.7 us; the launch traced here: 50.2 us
  Pallas kernels  49.6 us (98%)
  between operations  0.64 us (1%)
    pallas_call x1, Pallas kernels, per_device(): pl.pallas_call(kernel, out_shape=(jax.ShapeDtypeStruct((STEPS, 4 * HD), b...  48 us
    pallas_call x1, Pallas kernels, per_device(): pl.pallas_call(place, out_shape=(jax.ShapeDtypeStruct((STEPS, 4 * HD), bf...  1.58 us

profile of v5, /device:TPU:1, one launch (start us, length us, event | category | flops | bytes accessed | tf_op | source)
XLA Modules:
  0.0 50.2 jit_solution(16466977179105652533)
XLA Ops:
  0.6 48.0 %shard_map.95 = (bf16[64,512]{1,0:T(8,128)(2,1)}, bf16[128,128]{1,0:T(8,128)(2,1)}) custom-call(bf16[64,8192]{1,0:T(8,128)(2,1)} %bitcast.5, f32[1,8192]{1,0:T(1,128)} %bitcast.8, bf16[8192,512]{1,0:T(8,128)(2,1)} %wq_hbm.1, bf16[64,8192]{1,0:T(8,128)(2,1)} %bitcast.6, bf16[64,8192]{1,0:T(8,128)(2,1)} %bitcast.7, bf16[2,8,256,1024]{3,2,1,0:T(8,128)(2,1)} %kv_hbm.1, ...), custom_call_target="tpu_custom_call" | custom-call | tf_op jit(solution)/shard_map/pallas_call | solution.py:515
  48.7 1.6 %shard_map.96 = (bf16[64,512]{1,0:T(8,128)(2,1)}, bf16[1,1,16384]{2,1,0:T(2,128)(2,1)}) custom-call(bf16[64,512]{1,0:T(8,128)(2,1)} %get-tuple-element.6.att_ref, bf16[128,128]{1,0:T(8,128)(2,1)} %get-tuple-element.7.ent_ref), custom_call_target="tpu_custom_call" | custom-call | tf_op jit(solution)/shard_map/pallas_call | solution.py:575

commit v6 on v5

--- a/solution.py
+++ b/solution.py
@@ -376,8 +376,8 @@
                 device_id_type=MESH,
             ),
             pltpu.make_async_remote_copy(
-                src_ref=l_send.at[t, m],
-                dst_ref=l_buf.at[site],
+                src_ref=l_send.at[t, m, pl.ds(0, 1)],
+                dst_ref=l_buf.at[site, pl.ds(0, 1)],
                 send_sem=l_send_sem.at[t, m],
                 recv_sem=l_recv_sem.at[site],
                 device_id=home,
@@ -442,25 +442,26 @@
 
     lax.fori_loop(0, SLOTS, attend, 0)
 
-    def await_site(i, carry):
+    def await_site(i):
         @pl.when(jnp.logical_not(is_self(i)))
         def _():
             pltpu.make_async_copy(o_buf.at[i], o_buf.at[i], o_recv_sem.at[i]).wait()
-            pltpu.make_async_copy(l_buf.at[i], l_buf.at[i], l_recv_sem.at[i]).wait()
-
-        return carry
-
-    lax.fori_loop(0, SITES, await_site, 0)
-    top = own_l[pl.ds(0, 1), :]
-    for i in range(SITES):
-        top = jnp.maximum(top, l_buf[i, pl.ds(0, 1), :])
-    share = jnp.exp2(own_l[pl.ds(0, 1), :] - top)
-    total = share
-    result = own_o[...] * share
-    for i in range(SITES):
-        share = jnp.exp2(l_buf[i, pl.ds(0, 1), :] - top)
-        total = total + share
-        result = result + o_buf[i].astype(jnp.float32) * share
+            row = l_buf.at[i, pl.ds(0, 1)]
+            pltpu.make_async_copy(row, row, l_recv_sem.at[i]).wait()
+
+    top, total, result = own_l[pl.ds(0, 1), :], jnp.ones((1, GROUP), jnp.float32), own_o[...]
+    for sites in ((1, 3, 4, 5, 6, 7), (0, 2)):
+        for i in sites:
+            await_site(i)
+        old_top = top
+        for i in sites:
+            top = jnp.maximum(top, l_buf[i, pl.ds(0, 1), :])
+        share = jnp.exp2(old_top - top)
+        total, result = total * share, result * share
+        for i in sites:
+            share = jnp.exp2(l_buf[i, pl.ds(0, 1), :] - top)
+            total = total + share
+            result = result + o_buf[i].astype(jnp.float32) * share
     result = (result / total).T
     for g in range(4):
         att_ref[:, g * HD : (g + 1) * HD] = result[g * STEPS : (g + 1) * STEPS, :].astype(

time: 50.7 us -> 50.3 us (level)
  no operation moved by 1% of the time
where the time goes in v6:
time: 50.3 us; the launch traced here: 49.9 us
  Pallas kernels  49.2 us (98%)
  between operations  0.64 us (1%)
    pallas_call x1, Pallas kernels, per_device(): pl.pallas_call(kernel, out_shape=(jax.ShapeDtypeStruct((STEPS, 4 * HD), b...  47.7 us
    pallas_call x1, Pallas kernels, per_device(): pl.pallas_call(place, out_shape=(jax.ShapeDtypeStruct((STEPS, 4 * HD), bf...  1.58 us

profile of v6, /device:TPU:1, one launch (start us, length us, event | category | flops | bytes accessed | tf_op | source)
XLA Modules:
  0.0 49.9 jit_solution(17952953882566937222)
XLA Ops:
  0.6 47.7 %shard_map.95 = (bf16[64,512]{1,0:T(8,128)(2,1)}, bf16[128,128]{1,0:T(8,128)(2,1)}) custom-call(bf16[64,8192]{1,0:T(8,128)(2,1)} %bitcast.5, f32[1,8192]{1,0:T(1,128)} %bitcast.8, bf16[8192,512]{1,0:T(8,128)(2,1)} %wq_hbm.1, bf16[64,8192]{1,0:T(8,128)(2,1)} %bitcast.6, bf16[64,8192]{1,0:T(8,128)(2,1)} %bitcast.7, bf16[2,8,256,1024]{3,2,1,0:T(8,128)(2,1)} %kv_hbm.1, ...), custom_call_target="tpu_custom_call" | custom-call | tf_op jit(solution)/shard_map/pallas_call | solution.py:516
  48.3 1.6 %shard_map.96 = (bf16[64,512]{1,0:T(8,128)(2,1)}, bf16[1,1,16384]{2,1,0:T(2,128)(2,1)}) custom-call(bf16[64,512]{1,0:T(8,128)(2,1)} %get-tuple-element.6.att_ref, bf16[128,128]{1,0:T(8,128)(2,1)} %get-tuple-element.7.ent_ref), custom_call_target="tpu_custom_call" | custom-call | tf_op jit(solution)/shard_map/pallas_call | solution.py:576
